TPU v7x, 256 devices: a whole 4x4x8 slice. The times are simulated.
256 devices in a mesh: cgrp: 8 (over z), dev: 32 (over x, y, core).
Axes of the slice: x: 4, y: 4, z: 8, core: 2. Of those that a mesh axis runs over, the one named last changes fastest.
Arguments:
- docs: bfloat16 [65536, 1024], P('dev'), may hold values from -140 to 140
- centroids: float32 [8192, 1024], P(('cgrp', 'dev')), may hold values from -6 to 6
Outputs:
- centroids_next: float32 [8192, 1024], P(('cgrp', 'dev'))
- mass: float32 [8192], P(('cgrp', 'dev'))
- doc_lse: float32 [65536], P('dev')
All inputs are finite; a program needn't handle non-finite values.
Results may differ from a plain program's by a relative error of at most 0.012.
The roundings to bfloat16 on the way count: a program that leaves them out, or rounds other values in their place, can miss the bound.
Values may be sent and summed in bfloat16 or wider, within the bound.
A program may use at most 64 MiB of HBM per device.

v0:
```python
import math
import jax
import jax.numpy as jnp
from jax import lax
from jax.sharding import PartitionSpec as P


def body(docs, centroids):
    width = docs.shape[1]
    scale = 4.0 / math.sqrt(width)
    rounded = centroids.astype(jnp.bfloat16)
    gathered = lax.all_gather(rounded, "dev", axis=0, tiled=True)
    gathered_wide = gathered.astype(jnp.float32)
    gathered_norms = jnp.sum(gathered_wide * gathered_wide, axis=1)
    dots = lax.dot_general(
        docs, gathered, (((1,), (1,)), ((), ())), preferred_element_type=jnp.float32
    )
    scores = (dots - 0.5 * gathered_norms[None, :]) * scale
    local_max = jnp.max(scores, axis=1)
    local_sum = jnp.sum(jnp.exp(scores - local_max[:, None]), axis=1)
    group_top = lax.pmax(local_max, "cgrp")
    group_sum = lax.psum(local_sum * jnp.exp(local_max - group_top), "cgrp")
    doc_lse = group_top + jnp.log(group_sum)
    resp = jnp.exp(scores - doc_lse[:, None])
    docs_wide = docs.astype(jnp.float32)
    local_mass = jnp.sum(resp, axis=0)
    term = lax.dot_general(
        resp,
        docs_wide,
        (((0,), (0,)), ((), ())),
        preferred_element_type=jnp.float32,
        precision=lax.Precision.HIGHEST,
    )
    weighted, mass = (
        lax.psum_scatter(term, "dev", scatter_dimension=0, tiled=True),
        lax.psum_scatter(local_mass, "dev", scatter_dimension=0, tiled=True),
    )
    centroids_next = (weighted + centroids) / (mass[:, None] + 1.0)
    return (centroids_next, mass, doc_lse)


def solution(mesh):
    in_specs = (P("dev", None), P(("cgrp", "dev"), None))
    out_specs = (P(("cgrp", "dev"), None), P(("cgrp", "dev")), P("dev"))
    return jax.shard_map(body, mesh=mesh, in_specs=in_specs, out_specs=out_specs, check_vma=False)
```

profile of v0, /device:TPU:2, one launch (start us, length us, event | category | flops | bytes accessed | tf_op | source)
XLA Modules:
  0.0 227.5 jit_solution(16202654459003388817)
XLA Ops:
  7.2 0.0 all-gather.2.cloned.1.call-start
  7.2 1.5 convert_element_type.7
  8.8 0.0 all-gather.2.cloned.1.call-update
  8.8 0.0 reduce-scatter.2.cloned.1.call-start
  8.8 53.7 %all-gather.2.cloned.1.call-done = bf16[1024,1024]{1,0:T(8,128)(2,1)} async-done(((bf16[32,1024]{1,0:T(8,128)(2,1)}), bf16[1024,1024]{1,0:T(8,128)(2,1)}) %all-gather.2.cloned.1.call-update) | async-done | bytes 2097168 | tf_op jit(solution)/shard_map/all_gather | solution.py:12
  62.5 2.1 multiply_reduce_fusion
  64.6 10.6 %fusion.2 = (f32[2048]{0:T(1024)S(1)}, f32[2048,1024]{0,1:T(8,128)}) fusion(f32[1024]{0:T(1024)S(1)} %broadcast_multiply_fusion, bf16[2048,1024]{1,0:T(8,128)(2,1)} %param.2, bf16[1024,1024]{1,0:T(8,128)(2,1)} %all-gather.2.cloned.1.call-done), kind=kOutput, calls=%fused_computation.5 | convolution fusion | flops 4301256704 | bytes 14692352 | tf_op jit(solution)/shard_map/dot_general | solution.py:15
  75.2 17.7 %pmax.7 = f32[2048]{0:T(1024)S(1)} all-reduce(f32[2048]{0:T(1024)S(1)} %get-tuple-element.5), channel_id=1, replica_groups=mesh['cgrp'=8,'dev'=32] {'cgrp'}, use_global_device_ids=true, to_apply=%region_2.0 | all-reduce | flops 2048 | bytes 16384 | tf_op jit(solution)/shard_map/pmax | solution.py:21
  92.9 4.5 %exponential_reduce_fusion = f32[2048]{0:T(1024)S(1)} fusion(f32[2048,1024]{0,1:T(8,128)} %get-tuple-element.6, f32[2048]{0:T(1024)S(1)} %get-tuple-element.5, f32[1024]{0:T(1024)S(1)} %broadcast_multiply_fusion), kind=kLoop, calls=%fused_computation.1 | loop fusion | flops 8386560 | bytes 8409088 | tf_op jit(solution)/shard_map/reduce_sum | solution.py:20
  97.4 15.5 %psum.7 = f32[2048]{0:T(1024)S(1)} all-reduce(f32[2048]{0:T(1024)S(1)} %exponential_multiply_fusion), channel_id=1, replica_groups=mesh['cgrp'=8,'dev'=32] {'cgrp'}, use_global_device_ids=true, to_apply=%region_4.0 | all-reduce | flops 2048 | bytes 16384 | tf_op jit(solution)/shard_map/psum | solution.py:22
  112.9 0.0 copy-start.1
  112.9 0.0 copy-start.2
  113.0 19.1 %fusion.1 = f32[1024,1024]{1,0:T(8,128)} fusion(bf16[2048,1024]{1,0:T(8,128)(2,1)} %param.2, f32[2048,1024]{0,1:T(8,128)} %get-tuple-element.6, f32[2048]{0:T(1024)S(1)} %log_add_fusion, f32[1024]{0:T(1024)S(1)} %broadcast_multiply_fusion), kind=kOutput, calls=%fused_computation.4 | convolution fusion | flops 25776095232 | bytes 16789504 | tf_op jit(solution)/shard_map/dot_general | solution.py:27
  132.1 0.0 copy-start
  132.1 0.0 reduce-scatter.2.cloned.1.call-update
  132.1 0.0 copy-done.2
  132.1 0.6 dynamic-slice
  133.3 0.0 copy-done.1
  133.4 4.5 %fusion = f32[1024]{0:T(1024)S(1)} fusion(f32[2048,1024]{0,1:T(8,128)} %get-tuple-element.6, f32[2048]{0:T(1024)S(1)} %log_add_fusion, f32[1024]{0:T(1024)S(1)} %broadcast_multiply_fusion), kind=kLoop, calls=%fused_computation.3 | loop fusion | flops 8387584 | bytes 8404992 | tf_op jit(solution)/shard_map/reduce_sum | solution.py:26
  137.9 53.2 %all-reduce = f32[1024]{0:T(1024)S(1)} all-reduce(f32[1024]{0:T(1024)S(1)} %fusion), channel_id=3, replica_groups=mesh['cgrp'=8,'dev'=32] {'dev'}, use_global_device_ids=true, to_apply=%region_7.0.clone | all-reduce | flops 1024 | bytes 8192
  191.0 0.6 broadcast_add_fusion
  191.6 27.5 %reduce-scatter.2.cloned.1.call-done = f32[32,1024]{1,0:T(8,128)} async-done(((f32[1024,1024]{1,0:T(8,128)}), f32[32,1024]{1,0:T(8,128)}) %reduce-scatter.2.cloned.1.call-update) | async-done | bytes 131088 | tf_op jit(solution)/shard_map/reduce_scatter | solution.py:35
  219.1 0.0 copy-done
  219.1 1.6 add_divide_fusion
  (3 shorter events, 0.0 us)
Async XLA Ops:
  7.2 55.4 %all-gather.2.cloned.1.call-start = ((), (), s32[]{:S(2)}) async-start(), calls=%async_computation.1 | async-start | bytes 2162688 | tf_op jit(solution)/shard_map/all_gather | solution.py:12
  8.8 210.3 %reduce-scatter.2.cloned.1.call-start = ((), (), s32[]{:S(2)}) async-start(), calls=%async_computation.2 | async-start | bytes 4325376 | tf_op jit(solution)/shard_map/reduce_scatter | solution.py:35
  112.9 20.4 %copy-start.1 = (f32[2048]{0:T(1024)}, f32[2048]{0:T(1024)S(1)}, u32[]{:S(2)}) copy-start(f32[2048]{0:T(1024)S(1)} %log_add_fusion) | copy-start | bytes 24580
  112.9 19.2 %copy-start.2 = (u32[256]{0:T(256)S(1)}, u32[256]{0:T(256)}, u32[]{:S(2)}) copy-start(u32[256]{0:T(256)} %constant.13) | copy-start | bytes 3076
  132.1 87.0 %copy-start = (f32[32,1024]{1,0:T(8,128)S(1)}, f32[32,1024]{1,0:T(8,128)}, u32[]{:S(2)}) copy-start(f32[32,1024]{1,0:T(8,128)} %param.3) | copy-start | bytes 393220
Sparse Core Ops, SparseCore 0:
  11.1 51.3 all-gather.1
  132.2 86.8 reduce-scatter.1
where the time goes:
time: 228 us
  blocking collectives  86.3 us (38%)
  waiting for transfers between devices  81.2 us (36%)
  matrix products  29.7 us (13%)
  other arithmetic  14.9 us (7%)
  between operations  14.8 us (6%)
    all_gather x1, waiting for transfers between devices, body(): gathered = lax.all_gather(rounded, 'dev', axis=0, tiled=True)  53.7 us
    unnamed x1, blocking collectives  53.2 us
    reduce_scatter x1, waiting for transfers between devices, body(): lax.psum_scatter(term, 'dev', scatter_dimension=0, tiled=True)  27.5 us
    dot_general x1, matrix products, body(): lax.dot_general(resp, docs_wide, (((0,), (0,)), ((), ())), preferred_elem...  19.1 us
    pmax x1, blocking collectives, body(): group_top = lax.pmax(local_max, 'cgrp')  17.7 us
    psum x1, blocking collectives, body(): group_sum = lax.psum(local_sum * jnp.exp(local_max - group_top), 'cgrp')  15.5 us
    dot_general x1, matrix products, body(): lax.dot_general(docs, gathered, (((1,), (1,)), ((), ())), preferred_eleme...  10.6 us
  transfers between devices with their start and end apart: 2, of which 2 were waited for; matrix products, arithmetic and copies ran while one was open for 2% of the time, Pallas kernels for 0%

commit v1 on v0

--- a/solution.py
+++ b/solution.py
@@ -9,7 +9,10 @@
     width = docs.shape[1]
     scale = 4.0 / math.sqrt(width)
     rounded = centroids.astype(jnp.bfloat16)
-    gathered = lax.all_gather(rounded, "dev", axis=0, tiled=True)
+    n_dev = lax.axis_size("dev")
+    blocks = jnp.stack([rounded for _ in range(n_dev)])
+    blocks = lax.all_to_all(blocks, "dev", split_axis=0, concat_axis=0)
+    gathered = jnp.concatenate(blocks, axis=0)
     gathered_wide = gathered.astype(jnp.float32)
     gathered_norms = jnp.sum(gathered_wide * gathered_wide, axis=1)
     dots = lax.dot_general(

time: 228 us -> 205 us (0.90)
  waiting for transfers between devices: 81.2 us -> 27.8 us
  blocking collectives: 86.3 us -> 121 us
    all_gather x1 -> x0, waiting for transfers between devices: 53.7 us -> none  [body(): gathered = lax.all_gather(rounded, 'dev', axis=0, tiled=True)]
    all_to_all x0 -> x1, blocking collectives: none -> 33.1 us  [body(): blocks = lax.all_to_all(blocks, 'dev', split_axis=0, concat_axis=0)]
    pmax x1, blocking collectives: 17.7 us -> 20.3 us  [body(): group_top = lax.pmax(local_max, 'cgrp')]
  transfers between devices with their start and end apart: 2 -> 1, of which waited for: 2 -> 1; matrix products, arithmetic and copies ran while one was open for 2% -> 3% of each run, Pallas kernels for 0% -> 0%
where the time goes in v1:
time: 205 us
  blocking collectives  121 us (59%)
  matrix products  28 us (14%)
  waiting for transfers between devices  27.8 us (14%)
  between operations  14.8 us (7%)
  other arithmetic  12.7 us (6%)
    unnamed x1, blocking collectives  53.1 us
    all_to_all x1, blocking collectives, body(): blocks = lax.all_to_all(blocks, 'dev', split_axis=0, concat_axis=0)  33.1 us
    reduce_scatter x1, waiting for transfers between devices, body(): lax.psum_scatter(term, 'dev', scatter_dimension=0, tiled=True)  27.8 us
    pmax x1, blocking collectives, body(): group_top = lax.pmax(local_max, 'cgrp')  20.3 us
    dot_general x1, matrix products, body(): lax.dot_general(resp, docs_wide, (((0,), (0,)), ((), ())), preferred_elem...  19.1 us
    psum x1, blocking collectives, body(): group_sum = lax.psum(local_sum * jnp.exp(local_max - group_top), 'cgrp')  14.4 us
    dot_general x1, matrix products, body(): lax.dot_general(docs, gathered, (((1,), (1,)), ((), ())), preferred_eleme...  8.94 us
    reduce_sum x1, other arithmetic, body(): local_sum = jnp.sum(jnp.exp(scores - local_max[:, None]), axis=1)  4.51 us
  transfers between devices with their start and end apart: 1, of which 1 were waited for; matrix products, arithmetic and copies ran while one was open for 3% of the time, Pallas kernels for 0%

profile of v1, /device:TPU:2, one launch (start us, length us, event | category | flops | bytes accessed | tf_op | source)
XLA Modules:
  0.0 205.2 jit_solution(16600731884991146847)
XLA Ops:
  7.2 0.0 reduce-scatter.2.cloned.1.call-start
  7.2 0.9 convert_element_type.8
  8.1 0.2 stack.2
  8.4 33.1 %all_to_all.5 = bf16[32,32,1024]{2,1,0:T(8,128)(2,1)S(1)} all-to-all(bf16[32,32,1024]{2,1,0:T(8,128)(2,1)S(1)} %stack.2), channel_id=1, replica_groups=mesh['cgrp'=8,'dev'=32] {'dev'}, dimensions={0} | all-to-all | bytes 4194304 | tf_op jit(solution)/shard_map/all_to_all | solution.py:14
  41.5 0.5 multiply_reduce_fusion
  42.0 0.1 mul.30
  42.0 8.9 %fusion.2 = (f32[2048]{0:T(1024)S(1)}, f32[2048,1024]{0,1:T(8,128)}) fusion(f32[1024]{0:T(1024)S(1)} %mul.30, bf16[2048,1024]{1,0:T(8,128)(2,1)} %param.2, bf16[1024,1024]{1,0:T(8,128)(2,1)S(1)} %bitcast.5), kind=kOutput, calls=%fused_computation.5 | convolution fusion | flops 4301256704 | bytes 14692352 | tf_op jit(solution)/shard_map/dot_general | solution.py:18
  51.0 20.3 %pmax.7 = f32[2048]{0:T(1024)S(1)} all-reduce(f32[2048]{0:T(1024)S(1)} %get-tuple-element.5), channel_id=1, replica_groups=mesh['cgrp'=8,'dev'=32] {'cgrp'}, use_global_device_ids=true, to_apply=%region_2.0 | all-reduce | flops 2048 | bytes 16384 | tf_op jit(solution)/shard_map/pmax | solution.py:24
  71.2 4.5 %exponential_reduce_fusion = f32[2048]{0:T(1024)S(1)} fusion(f32[2048,1024]{0,1:T(8,128)} %get-tuple-element.6, f32[2048]{0:T(1024)S(1)} %get-tuple-element.5, f32[1024]{0:T(1024)S(1)} %mul.30), kind=kLoop, calls=%fused_computation.1 | loop fusion | flops 8386560 | bytes 8409088 | tf_op jit(solution)/shard_map/reduce_sum | solution.py:23
  75.8 14.4 %psum.7 = f32[2048]{0:T(1024)S(1)} all-reduce(f32[2048]{0:T(1024)S(1)} %exponential_multiply_fusion), channel_id=1, replica_groups=mesh['cgrp'=8,'dev'=32] {'cgrp'}, use_global_device_ids=true, to_apply=%region_4.0 | all-reduce | flops 2048 | bytes 16384 | tf_op jit(solution)/shard_map/psum | solution.py:25
  90.2 0.0 copy-start.1
  90.2 0.0 copy-start.2
  90.2 19.1 %fusion.1 = f32[1024,1024]{1,0:T(8,128)} fusion(bf16[2048,1024]{1,0:T(8,128)(2,1)} %param.2, f32[2048,1024]{0,1:T(8,128)} %get-tuple-element.6, f32[2048]{0:T(1024)S(1)} %log_add_fusion, f32[1024]{0:T(1024)S(1)} %mul.30), kind=kOutput, calls=%fused_computation.4 | convolution fusion | flops 25776095232 | bytes 16789504 | tf_op jit(solution)/shard_map/dot_general | solution.py:30
  109.3 0.0 copy-start
  109.3 0.0 reduce-scatter.2.cloned.1.call-update
  109.4 0.0 copy-done.2
  109.4 0.6 dynamic-slice
  110.6 0.0 copy-done.1
  110.6 4.5 %fusion = f32[1024]{0:T(1024)S(1)} fusion(f32[2048,1024]{0,1:T(8,128)} %get-tuple-element.6, f32[2048]{0:T(1024)S(1)} %log_add_fusion, f32[1024]{0:T(1024)S(1)} %mul.30), kind=kLoop, calls=%fused_computation.3 | loop fusion | flops 8387584 | bytes 8404992 | tf_op jit(solution)/shard_map/reduce_sum | solution.py:29
  115.1 53.1 %all-reduce = f32[1024]{0:T(1024)S(1)} all-reduce(f32[1024]{0:T(1024)S(1)} %fusion), channel_id=3, replica_groups=mesh['cgrp'=8,'dev'=32] {'dev'}, use_global_device_ids=true, to_apply=%region_7.0.clone | all-reduce | flops 1024 | bytes 8192
  168.3 0.6 broadcast_add_fusion
  168.9 27.8 %reduce-scatter.2.cloned.1.call-done = f32[32,1024]{1,0:T(8,128)} async-done(((f32[1024,1024]{1,0:T(8,128)}), f32[32,1024]{1,0:T(8,128)}) %reduce-scatter.2.cloned.1.call-update) | async-done | bytes 131088 | tf_op jit(solution)/shard_map/reduce_scatter | solution.py:38
  196.7 0.0 copy-done
  196.7 1.6 add_divide_fusion
  (3 shorter events, 0.0 us)
Async XLA Ops:
  7.2 189.5 %reduce-scatter.2.cloned.1.call-start = ((), (), s32[]{:S(2)}) async-start(), calls=%async_computation.2 | async-start | bytes 4325376 | tf_op jit(solution)/shard_map/reduce_scatter | solution.py:38
  90.2 20.4 %copy-start.1 = (f32[2048]{0:T(1024)}, f32[2048]{0:T(1024)S(1)}, u32[]{:S(2)}) copy-start(f32[2048]{0:T(1024)S(1)} %log_add_fusion) | copy-start | bytes 24580
  90.2 19.2 %copy-start.2 = (u32[256]{0:T(256)S(1)}, u32[256]{0:T(256)}, u32[]{:S(2)}) copy-start(u32[256]{0:T(256)} %constant.13) | copy-start | bytes 3076
  109.3 87.3 %copy-start = (f32[32,1024]{1,0:T(8,128)S(1)}, f32[32,1024]{1,0:T(8,128)}, u32[]{:S(2)}) copy-start(f32[32,1024]{1,0:T(8,128)} %param.3) | copy-start | bytes 393220
Sparse Core Ops, SparseCore 0:
  109.5 87.1 reduce-scatter.1

commit v2 on v0

--- a/solution.py
+++ b/solution.py
@@ -19,7 +19,9 @@
     local_max = jnp.max(scores, axis=1)
     local_sum = jnp.sum(jnp.exp(scores - local_max[:, None]), axis=1)
     group_top = lax.pmax(local_max, "cgrp")
-    group_sum = lax.psum(local_sum * jnp.exp(local_max - group_top), "cgrp")
+    part = local_sum * jnp.exp(local_max - group_top)
+    parts = lax.all_gather(part, "cgrp")
+    group_sum = jnp.sum(parts, axis=0)
     doc_lse = group_top + jnp.log(group_sum)
     resp = jnp.exp(scores - doc_lse[:, None])
     docs_wide = docs.astype(jnp.float32)

time: 228 us -> 237 us (1.039)
  blocking collectives: 86.3 us -> 95.7 us
    all_gather x0 -> x1, blocking collectives: none -> 24.7 us  [body(): parts = lax.all_gather(part, 'cgrp')]
    psum x1 -> x0, blocking collectives: 15.5 us -> none  [body(): group_sum = lax.psum(local_sum * jnp.exp(local_max - group_top), 'cgrp')]
where the time goes in v2:
time: 237 us; the launch traced here: 236 us
  blocking collectives  95.7 us (40%)
  waiting for transfers between devices  80.6 us (34%)
  matrix products  29.7 us (13%)
  other arithmetic  14.9 us (6%)
  between operations  14.8 us (6%)
    all_gather x1, waiting for transfers between devices, body(): gathered = lax.all_gather(rounded, 'dev', axis=0, tiled=True)  53.7 us
    unnamed x1, blocking collectives  53.2 us
    reduce_scatter x1, waiting for transfers between devices, body(): lax.psum_scatter(term, 'dev', scatter_dimension=0, tiled=True)  26.9 us
    all_gather x1, blocking collectives, body(): parts = lax.all_gather(part, 'cgrp')  24.7 us
    dot_general x1, matrix products, body(): lax.dot_general(resp, docs_wide, (((0,), (0,)), ((), ())), preferred_elem...  19.1 us
    pmax x1, blocking collectives, body(): group_top = lax.pmax(local_max, 'cgrp')  17.7 us
    dot_general x1, matrix products, body(): lax.dot_general(docs, gathered, (((1,), (1,)), ((), ())), preferred_eleme...  10.6 us
  transfers between devices with their start and end apart: 2, of which 2 were waited for; matrix products, arithmetic and copies ran while one was open for 2% of the time, Pallas kernels for 0%

profile of v2, /device:TPU:2, one launch (start us, length us, event | category | flops | bytes accessed | tf_op | source)
XLA Modules:
  0.0 236.4 jit_solution(15914247017447422261)
XLA Ops:
  7.2 0.0 all-gather.3.cloned.1.call-start
  7.2 1.5 convert_element_type.7
  8.8 0.0 all-gather.3.cloned.1.call-update
  8.8 0.0 reduce-scatter.2.cloned.1.call-start
  8.8 53.7 %all-gather.3.cloned.1.call-done = bf16[1024,1024]{1,0:T(8,128)(2,1)} async-done(((bf16[32,1024]{1,0:T(8,128)(2,1)}), bf16[1024,1024]{1,0:T(8,128)(2,1)}) %all-gather.3.cloned.1.call-update) | async-done | bytes 2097168 | tf_op jit(solution)/shard_map/all_gather | solution.py:12
  62.5 2.1 multiply_reduce_fusion
  64.6 10.6 %fusion.2 = (f32[2048]{0:T(1024)S(1)}, f32[2048,1024]{0,1:T(8,128)}) fusion(f32[1024]{0:T(1024)S(1)} %broadcast_multiply_fusion, bf16[2048,1024]{1,0:T(8,128)(2,1)} %param.2, bf16[1024,1024]{1,0:T(8,128)(2,1)} %all-gather.3.cloned.1.call-done), kind=kOutput, calls=%fused_computation.5 | convolution fusion | flops 4301256704 | bytes 14692352 | tf_op jit(solution)/shard_map/dot_general | solution.py:15
  75.2 17.7 %pmax.7 = f32[2048]{0:T(1024)S(1)} all-reduce(f32[2048]{0:T(1024)S(1)} %get-tuple-element.5), channel_id=1, replica_groups=mesh['cgrp'=8,'dev'=32] {'cgrp'}, use_global_device_ids=true, to_apply=%region_2.0 | all-reduce | flops 2048 | bytes 16384 | tf_op jit(solution)/shard_map/pmax | solution.py:21
  92.9 4.5 %exponential_reduce_fusion = f32[2048]{0:T(1024)S(1)} fusion(f32[2048,1024]{0,1:T(8,128)} %get-tuple-element.6, f32[2048]{0:T(1024)S(1)} %get-tuple-element.5, f32[1024]{0:T(1024)S(1)} %broadcast_multiply_fusion), kind=kLoop, calls=%fused_computation.1 | loop fusion | flops 8386560 | bytes 8409088 | tf_op jit(solution)/shard_map/reduce_sum | solution.py:20
  97.4 24.7 %all-gather = f32[16384]{0:T(1024)S(1)} all-gather(f32[2048]{0:T(1024)S(1)} %exponential_multiply_fusion), channel_id=2, replica_groups=mesh['cgrp'=8,'dev'=32] {'cgrp'}, dimensions={0}, use_global_device_ids=true | all-gather | bytes 73728 | tf_op jit(solution)/shard_map/all_gather | solution.py:23
  122.2 0.0 copy-start.1
  122.3 0.0 copy-start.2
  122.3 19.1 %fusion.1 = f32[1024,1024]{1,0:T(8,128)} fusion(bf16[2048,1024]{1,0:T(8,128)(2,1)} %param.2, f32[2048,1024]{0,1:T(8,128)} %get-tuple-element.6, f32[2048]{0:T(1024)S(1)} %log_add_fusion, f32[1024]{0:T(1024)S(1)} %broadcast_multiply_fusion), kind=kOutput, calls=%fused_computation.4 | convolution fusion | flops 25776095232 | bytes 16789504 | tf_op jit(solution)/shard_map/dot_general | solution.py:29
  141.4 0.0 copy-start
  141.4 0.0 reduce-scatter.2.cloned.1.call-update
  141.4 0.0 copy-done.2
  141.4 0.6 dynamic-slice
  142.7 0.0 copy-done.1
  142.7 4.5 %fusion = f32[1024]{0:T(1024)S(1)} fusion(f32[2048,1024]{0,1:T(8,128)} %get-tuple-element.6, f32[2048]{0:T(1024)S(1)} %log_add_fusion, f32[1024]{0:T(1024)S(1)} %broadcast_multiply_fusion), kind=kLoop, calls=%fused_computation.3 | loop fusion | flops 8387584 | bytes 8404992 | tf_op jit(solution)/shard_map/reduce_sum | solution.py:28
  147.2 53.2 %all-reduce = f32[1024]{0:T(1024)S(1)} all-reduce(f32[1024]{0:T(1024)S(1)} %fusion), channel_id=4, replica_groups=mesh['cgrp'=8,'dev'=32] {'dev'}, use_global_device_ids=true, to_apply=%region_7.0.clone | all-reduce | flops 1024 | bytes 8192
  200.4 0.6 broadcast_add_fusion
  201.0 26.9 %reduce-scatter.2.cloned.1.call-done = f32[32,1024]{1,0:T(8,128)} async-done(((f32[1024,1024]{1,0:T(8,128)}), f32[32,1024]{1,0:T(8,128)}) %reduce-scatter.2.cloned.1.call-update) | async-done | bytes 131088 | tf_op jit(solution)/shard_map/reduce_scatter | solution.py:37
  227.9 0.0 copy-done
  227.9 1.6 add_divide_fusion
  (5 shorter events, 0.1 us)
Async XLA Ops:
  7.2 55.4 %all-gather.3.cloned.1.call-start = ((), (), s32[]{:S(2)}) async-start(), calls=%async_computation.1 | async-start | bytes 2162688 | tf_op jit(solution)/shard_map/all_gather | solution.py:12
  8.8 219.1 %reduce-scatter.2.cloned.1.call-start = ((), (), s32[]{:S(2)}) async-start(), calls=%async_computation.2 | async-start | bytes 4325376 | tf_op jit(solution)/shard_map/reduce_scatter | solution.py:37
  122.2 20.4 %copy-start.1 = (f32[2048]{0:T(1024)}, f32[2048]{0:T(1024)S(1)}, u32[]{:S(2)}) copy-start(f32[2048]{0:T(1024)S(1)} %log_add_fusion) | copy-start | bytes 24580
  122.3 19.2 %copy-start.2 = (u32[256]{0:T(256)S(1)}, u32[256]{0:T(256)}, u32[]{:S(2)}) copy-start(u32[256]{0:T(256)} %constant.13) | copy-start | bytes 3076
  141.4 86.5 %copy-start = (f32[32,1024]{1,0:T(8,128)S(1)}, f32[32,1024]{1,0:T(8,128)}, u32[]{:S(2)}) copy-start(f32[32,1024]{1,0:T(8,128)} %param.3) | copy-start | bytes 393220
Sparse Core Ops, SparseCore 0:
  11.1 51.3 all-gather.2
  141.5 86.3 reduce-scatter.1
